TPU v7x, 32 devices: a whole 2x2x4 slice. The times are simulated.
32 devices in a mesh: seq: 4 (over z), batch: 4 (over y, x), tp: 2 (over core).
Axes of the slice: x: 2, y: 2, z: 4, core: 2. Of those that a mesh axis runs over, the one named last changes fastest.
Arguments:
- pre_q: bfloat16 [4, 512, 4096], P('batch', 'seq', 'tp'), may hold values from -40 to 40
- pre_k: bfloat16 [4, 512, 512], P('batch', 'seq', 'tp'), may hold values from -40 to 40
- pre_v: bfloat16 [4, 512, 512], P('batch', 'seq', 'tp'), may hold values from -12 to 12
- owner_map: int32 [4, 32, 1], P('batch', 'seq'), may hold values from 0 to 3; in each aligned block of 8 rows (0 to 7, 8 to 15, ..., all dimensions but the last counted through in order) at most 4 rows name the same one
- cache_k: bfloat16 [32, 64, 512], P('batch', 'seq', 'tp'), may hold values from -6 to 6
- cache_v: bfloat16 [32, 64, 512], P('batch', 'seq', 'tp'), may hold values from -12 to 12
- tables: int32 [8, 16], P('batch', 'seq'), may hold values from 0 to 7, as said below
- lengths: int32 [8], P('batch'), may hold values from 1 to 256, 1024 in all
- dec_q: float32 [8, 3, 4096], P('batch', None, 'tp'), may hold values from -40 to 40
- dec_k: float32 [8, 3, 512], P('batch', None, 'tp'), may hold values from -40 to 40
- dec_v: float32 [8, 3, 512], P('batch', None, 'tp'), may hold values from -12 to 12
- w_out: bfloat16 [4096, 8192], P('tp', 'seq'), may hold values from -0.09375 to 0.09375
Outputs:
- pre_out: bfloat16 [4, 512, 4096], P('batch', 'seq', 'tp')
- dec_out: float32 [8, 3, 8192], P('batch', None, 'seq')
Inputs may be any that keep to these rules, and one draw needn't show every extreme that they name: `owner_map`: in each aligned block of 8 rows (the pages of one index of seq of one span) no owner is named more than 4 times. `tables`: within one owner's 2 requests and one index of seq, the 8 entries are distinct.
All inputs are finite; a program needn't handle non-finite values. No bound on the sum of `lengths` on one device may be relied on, other than what follows from the above.
Results may differ from a plain program's by a relative error of at most 0.0033.
Values may be sent and summed in bfloat16 or wider, within the bound.
A program may use at most 64 MiB of HBM per device.

v0:
```python
import jax
import jax.numpy as jnp
from jax import lax
from jax.sharding import PartitionSpec as P

HD = 128


highest = lax.Precision.HIGHEST
floor_score = -1e30


def merged(value, axis, combine):
    everything = jax.tree.map(lambda part: lax.all_gather(part, axis), value)
    leading = jax.tree.map(lambda part: part[0], everything)

    def step(k, so_far):
        return combine(so_far, jax.tree.map(lambda part: part[k], everything))

    return lax.fori_loop(1, lax.axis_size(axis), step, leading)


def block_math(query_block, key_rows, value_rows, start_row):
    block_rows = query_block.shape[0]
    key_count = key_rows.shape[0]
    scaling = HD ** (-0.5)
    scores = (
        jnp.einsum("qagd,kad->agqk", query_block, key_rows, preferred_element_type=jnp.float32)
        * scaling
    )
    query_pos = start_row + jnp.arange(block_rows)
    visible = jnp.arange(key_count)[None, :] <= query_pos[:, None]
    masked = jnp.where(visible, scores, floor_score)
    row_peak = jnp.max(masked, axis=-1, keepdims=True)
    weights = jnp.where(visible, jnp.exp(scores - row_peak), 0.0)
    row_total = jnp.sum(weights, axis=-1)
    mixture = jnp.einsum(
        "agqk,kad->qagd",
        weights.astype(jnp.bfloat16),
        value_rows,
        preferred_element_type=jnp.float32,
    )
    return (mixture / jnp.transpose(row_total, (2, 0, 1))[..., None]).astype(jnp.bfloat16)


def attend_whole(queries, key_rows, value_rows):
    row_count = queries.shape[0]
    block_rows = min(512, row_count)
    pieces = []
    for block_id in range(row_count // block_rows):
        end_row = (block_id + 1) * block_rows
        pieces.append(
            block_math(
                queries[block_id * block_rows : end_row],
                key_rows[:end_row],
                value_rows[:end_row],
                block_id * block_rows,
            )
        )
    return jnp.concatenate(pieces, axis=0)


def partial_state(scores, visible, value_rows, pattern):
    masked = jnp.where(visible, scores, floor_score)
    row_peak = jnp.max(masked, axis=-1)
    weights = jnp.where(visible, jnp.exp(scores - row_peak[..., None]), 0.0)
    return (
        row_peak,
        jnp.sum(weights, axis=-1),
        jnp.einsum(pattern, weights, value_rows, precision=highest),
    )


def combine(first_state, second_state):
    row_peak = jnp.maximum(first_state[0], second_state[0])
    first_scale = jnp.exp(first_state[0] - row_peak)
    second_scale = jnp.exp(second_state[0] - row_peak)
    return (
        row_peak,
        first_state[1] * first_scale + second_state[1] * second_scale,
        first_state[2] * first_scale[..., None] + second_state[2] * second_scale[..., None],
    )


def shared_state(dec_queries, key_rows, value_rows, kept_rows):
    scores = jnp.einsum("rnkgd,tkd->rnkgt", dec_queries, key_rows, precision=highest) * HD ** (-0.5)
    return partial_state(scores, kept_rows, value_rows, "rnkgt,tkd->rnkgd")


def local(
    pre_q, pre_k, pre_v, owner_map, cache_k, cache_v, tables, lengths, dec_q, dec_k, dec_v, w_out
):
    seq_count = lax.axis_size("seq")
    seq_index = lax.axis_index("seq")
    bat_index = lax.axis_index("batch")
    tok_rows = pre_q.shape[1]
    q_heads = pre_q.shape[2] // HD
    k_heads = pre_k.shape[2] // HD
    group_size = q_heads // k_heads
    span_rows = tok_rows * seq_count
    queries = pre_q[0]
    key_rows = pre_k[0]
    value_rows = pre_v[0]
    per_device = q_heads // seq_count
    wide_q = queries.reshape(tok_rows, seq_count, per_device, HD)
    wide_k = jnp.repeat(key_rows.reshape(tok_rows, k_heads, HD), group_size, axis=1).reshape(
        tok_rows, seq_count, per_device, HD
    )
    wide_v = jnp.repeat(value_rows.reshape(tok_rows, k_heads, HD), group_size, axis=1).reshape(
        tok_rows, seq_count, per_device, HD
    )
    head_q = lax.all_to_all(wide_q, "seq", split_axis=1, concat_axis=0, tiled=True)
    head_k = lax.all_to_all(wide_k, "seq", split_axis=1, concat_axis=0, tiled=True)
    head_v = lax.all_to_all(wide_v, "seq", split_axis=1, concat_axis=0, tiled=True)
    head_count = head_q.shape[2]
    result = attend_whole(
        head_q.reshape(span_rows, head_count, 1, HD),
        head_k.reshape(span_rows, head_count, HD),
        head_v.reshape(span_rows, head_count, HD),
    )
    by_head = result.reshape(span_rows, 1, head_count, HD)
    prefill_rows = lax.all_to_all(by_head, "seq", split_axis=0, concat_axis=1, tiled=True).reshape(
        tok_rows, q_heads * HD
    )
    requests = dec_q.shape[0]
    new_count = dec_q.shape[1]
    dec_queries = dec_q.reshape(requests, new_count, k_heads, group_size, HD)
    table_count = tables.shape[1]
    page_rows = cache_k.shape[1]
    cached_k = (
        cache_k[tables].astype(jnp.float32).reshape(requests, table_count * page_rows, k_heads, HD)
    )
    cached_v = (
        cache_v[tables].astype(jnp.float32).reshape(requests, table_count * page_rows, k_heads, HD)
    )
    positions = (
        (jnp.arange(table_count)[:, None] * seq_count + seq_index) * page_rows
        + jnp.arange(page_rows)[None, :]
    ).reshape(-1)
    live_rows = (positions[None, :] < lengths[:, None])[:, None, None, None, :]
    scores = jnp.einsum("rnkgd,rtkd->rnkgt", dec_queries, cached_k, precision=highest) * HD ** (
        -0.5
    )
    partial_value = partial_state(scores, live_rows, cached_v, "rnkgt,rtkd->rnkgd")
    page_count = tok_rows // page_rows
    own_k = key_rows.reshape(page_count, page_rows, k_heads * HD)
    own_v = value_rows.reshape(page_count, page_rows, k_heads * HD)
    owners = owner_map[0, :, 0]
    piece_k = lax.all_gather(own_k, "batch", axis=0, tiled=True)
    piece_v = lax.all_gather(own_v, "batch", axis=0, tiled=True)
    piece_owner = lax.all_gather(owners.astype(jnp.bfloat16), "batch", axis=0, tiled=True)
    piece_pages = piece_k.shape[0]
    kept_rows = jnp.repeat(
        piece_owner.astype(jnp.float32) == bat_index.astype(jnp.float32), page_rows
    )
    fresh = shared_state(
        dec_queries,
        piece_k.astype(jnp.float32).reshape(piece_pages * page_rows, k_heads, HD),
        piece_v.astype(jnp.float32).reshape(piece_pages * page_rows, k_heads, HD),
        kept_rows,
    )
    partial_value = combine(partial_value, fresh)
    partial_value = merged(partial_value, "seq", combine)
    new_k = dec_k.reshape(requests, new_count, k_heads, HD)
    new_v = dec_v.reshape(requests, new_count, k_heads, HD)
    scores = jnp.einsum("rnkgd,rjkd->rnkgj", dec_queries, new_k, precision=highest) * HD ** (-0.5)
    causal = (jnp.arange(new_count)[None, :] <= jnp.arange(new_count)[:, None])[
        None, :, None, None, :
    ]
    partial_value = combine(
        partial_value, partial_state(scores, causal, new_v, "rnkgj,rjkd->rnkgd")
    )
    attention = (partial_value[2] / partial_value[1][..., None]).reshape(
        requests * new_count, q_heads * HD
    )
    projected = jnp.dot(attention, w_out.astype(jnp.float32), precision=highest)
    dec_out = lax.psum(projected, "tp").reshape(requests, new_count, projected.shape[1])
    return (prefill_rows[None], dec_out)


def solution(mesh):
    placed = (
        P("batch", "seq", "tp"),
        P("batch", "seq", "tp"),
        P("batch", "seq", "tp"),
        P("batch", "seq", None),
        P("batch", "seq", "tp"),
        P("batch", "seq", "tp"),
        P("batch", "seq"),
        P("batch"),
        P("batch", None, "tp"),
        P("batch", None, "tp"),
        P("batch", None, "tp"),
        P("tp", "seq"),
    )
    return jax.shard_map(
        local,
        mesh=mesh,
        in_specs=placed,
        out_specs=(P("batch", "seq", "tp"), P("batch", None, "seq")),
        check_vma=False,
    )
```

profile of v0, /device:TPU:26, one launch (start us, length us, event | category | flops | bytes accessed | tf_op | source)
XLA Modules:
  0.0 141.1 jit_solution(17257343757937576019)
XLA Ops:
  0.7 0.8 convert_bitcast_fusion
  1.5 1.3 copy.100
  2.8 1.0 copy.101
  3.8 1.2 dynamic-slice
  5.7 0.2 dynamic-update-slice
  6.0 5.1 %all-to-all-start.1 = ((bf16[128,4,4,128]{3,0,2,1:T(8,128)(2,1)}), bf16[128,4,4,128]{3,0,2,1:T(8,128)(2,1)S(1)}, u32[]{:S(2)}, u32[]{:S(2)}) async-start(bf16[128,4,4,128]{3,0,2,1:T(8,128)(2,1)} %copy.101), calls=%async_computation.1 | async-start | bytes 1048576 | tf_op jit(solution)/shard_map/all_to_all | solution.py:112
  11.1 8.0 %all-reduce = bf16[32]{0:T(256)(128)(2,1)S(1)} all-reduce(bf16[32]{0:T(256)(128)(2,1)S(1)} %dynamic-update-slice), channel_id=2, replica_groups=mesh['seq'=4,'batch'=4,'tp'=2] {'batch'}, use_global_device_ids=true, to_apply=%add | all-reduce | flops 32 | bytes 128
  19.2 0.1 reshape.205
  19.3 0.8 reshape.204
  20.1 0.9 reshape_squeeze.15
  21.0 9.9 %all_gather.24 = bf16[32,16,256]{2,1,0:T(8,128)(2,1)S(1)} all-gather(bf16[8,16,256]{2,1,0:T(8,128)(2,1)} %bitcast.181), channel_id=1, replica_groups=mesh['seq'=4,'batch'=4,'tp'=2] {'batch'}, dimensions={0}, use_global_device_ids=true | all-gather | bytes 327680 | tf_op jit(solution)/shard_map/all_gather | solution.py:149
  31.0 0.1 add.116
  31.1 0.1 reshape.215
  31.2 0.6 gather_fusion
  31.8 0.5 select_reduce_fusion
  32.2 0.2 fusion.65
  32.5 0.3 select_reduce_fusion.1
  32.9 8.3 %all_gather.27 = bf16[32,16,256]{2,1,0:T(8,128)(2,1)S(1)} all-gather(bf16[8,16,256]{2,1,0:T(8,128)(2,1)S(1)} %bitcast.182), channel_id=1, replica_groups=mesh['seq'=4,'batch'=4,'tp'=2] {'batch'}, dimensions={0}, use_global_device_ids=true | all-gather | bytes 327680 | tf_op jit(solution)/shard_map/all_gather | solution.py:150
  41.3 0.6 gather_fusion.1
  41.8 0.2 fusion.25
  42.1 0.3 fusion.23
  42.4 13.7 %all-gather.1 = f32[8,3,2,8,128]{4,3,2,1,0:T(8,128)S(1)} all-gather(f32[2,3,2,8,128]{4,3,2,1,0:T(8,128)S(1)} %copy.121), channel_id=3, replica_groups=mesh['seq'=4,'batch'=4,'tp'=2] {'seq'}, dimensions={0}, use_global_device_ids=true | all-gather | bytes 245760 | tf_op jit(solution)/shard_map/all_gather | solution.py:14
  56.1 0.2 fusion.40
  56.3 13.1 %all_gather.26 = f32[4,2,3,2,8]{4,3,2,1,0:T(2,128)S(1)} all-gather(f32[1,2,3,2,8]{4,3,2,1,0:T(2,128)S(1)} %get-tuple-element.228), channel_id=1, replica_groups=mesh['seq'=4,'batch'=4,'tp'=2] {'seq'}, dimensions={0}, use_global_device_ids=true | all-gather | bytes 1920 | tf_op jit(solution)/shard_map/all_gather | solution.py:14
  69.5 13.3 %all_gather.25 = f32[4,2,3,2,8]{4,3,2,1,0:T(2,128)S(1)} all-gather(f32[1,2,3,2,8]{4,3,2,1,0:T(2,128)S(1)} %get-tuple-element.229), channel_id=1, replica_groups=mesh['seq'=4,'batch'=4,'tp'=2] {'seq'}, dimensions={0}, use_global_device_ids=true | all-gather | bytes 1920 | tf_op jit(solution)/shard_map/all_gather | solution.py:14
  82.9 0.9 broadcast_in_dim.113
  83.8 5.1 %all-to-all-start = ((bf16[128,4,4,128]{3,0,2,1:T(8,128)(2,1)}), bf16[128,4,4,128]{3,0,2,1:T(8,128)(2,1)S(1)}, u32[]{:S(2)}, u32[]{:S(2)}) async-start(bf16[128,4,4,128]{3,0,2,1:T(8,128)(2,1)} %broadcast_in_dim.113), calls=%async_computation | async-start | bytes 1048576 | tf_op jit(solution)/shard_map/all_to_all | solution.py:113
  88.8 0.5 while.19
  88.9 0.1 fusion.75
  89.0 0.1 fusion.75
  89.2 0.1 fusion.75
  89.3 10.6 %all-to-all-done = bf16[128,4,4,128]{3,0,2,1:T(8,128)(2,1)S(1)} async-done(((bf16[128,4,4,128]{3,0,2,1:T(8,128)(2,1)}), bf16[128,4,4,128]{3,0,2,1:T(8,128)(2,1)S(1)}, u32[]{:S(2)}, u32[]{:S(2)}) %all-to-all-start) | async-done | bytes 524320 | tf_op jit(solution)/shard_map/all_to_all | solution.py:113
  99.9 0.9 broadcast_in_dim.118
  100.8 5.8 %all-to-all-start.2 = ((bf16[128,4,4,128]{3,0,2,1:T(8,128)(2,1)}), bf16[128,4,4,128]{3,0,2,1:T(8,128)(2,1)S(1)}, u32[]{:S(2)}, u32[]{:S(2)}) async-start(bf16[128,4,4,128]{3,0,2,1:T(8,128)(2,1)} %broadcast_in_dim.118), calls=%async_computation.2 | async-start | bytes 1048576 | tf_op jit(solution)/shard_map/all_to_all | solution.py:114
  106.6 0.6 select_reduce_fusion.2
  107.2 0.1 fusion.44
  107.5 11.6 %all-to-all-done.2 = bf16[128,4,4,128]{3,0,2,1:T(8,128)(2,1)S(1)} async-done(((bf16[128,4,4,128]{3,0,2,1:T(8,128)(2,1)}), bf16[128,4,4,128]{3,0,2,1:T(8,128)(2,1)S(1)}, u32[]{:S(2)}, u32[]{:S(2)}) %all-to-all-start.2) | async-done | bytes 524320 | tf_op jit(solution)/shard_map/all_to_all | solution.py:114
  119.2 0.9 fusion.3
  120.1 0.9 fusion.6
  121.0 1.4 %fusion.29 = bf16[512,1,4,128]{3,0,2,1:T(8,128)(2,1)S(1)} fusion(bf16[512,4,128]{2,0,1:T(8,128)(2,1)S(1)} %bitcast.180, f32[4,512,512]{2,1,0:T(8,128)S(1)} %get-tuple-element.231, f32[4,512]{1,0:T(4,128)S(1)} %get-tuple-element.230, pred[512,512]{0,1:T(8,128)(4,1)S(1)} %iota_compare_fusion, f32[512,4]{0,1:T(4,128)S(1)} %bitcast.186), kind=kOutput, calls=%fused_computation.41 | convolution fusion | flops 273154048 | bytes 5521408 | tf_op jit(solution)/shard_map/agqk,kad->qagd/dot_general | solution.py:37
  122.4 1.2 copy.106
  123.6 5.8 %all-to-all-start.3 = ((bf16[512,1,4,128]{3,2,1,0:T(4,128)(2,1)}), bf16[512,1,4,128]{3,2,1,0:T(4,128)(2,1)S(1)}, u32[]{:S(2)}, u32[]{:S(2)}) async-start(bf16[512,1,4,128]{3,2,1,0:T(4,128)(2,1)} %copy.106), calls=%async_computation.3 | async-start | bytes 1048576 | tf_op jit(solution)/shard_map/all_to_all | solution.py:122
  129.4 0.4 fusion.21
  129.8 5.7 %fusion.66 = f32[6,2048]{1,0:T(8,128)S(1)} fusion(f32[6,2048]{1,0:T(8,128)S(1)} %reshape.211, bf16[2048,2048]{1,0:T(8,128)(2,1)} %param.25), kind=kOutput, calls=%fused_computation.100 | convolution fusion | flops 301989888 | bytes 8486912 | tf_op jit(solution)/shard_map/dot_general | solution.py:176
  135.5 3.6 %psum.7 = f32[2,3,2048]{2,1,0:T(4,128)S(1)} all-reduce(f32[2,3,2048]{2,1,0:T(4,128)S(1)} %reshape.212), channel_id=1, replica_groups=mesh['seq'=4,'batch'=4,'tp'=2] {'tp'}, use_global_device_ids=true, to_apply=%region_10.11 | all-reduce | flops 12288 | bytes 98304 | tf_op jit(solution)/shard_map/psum | solution.py:177
  139.1 0.7 copy.130
  139.8 0.2 copy.107
  139.9 1.2 broadcast_in_dim_reshape.4
  (53 shorter events, 1.0 us)
Async XLA Ops:
  0.6 30.6 %copy-start = (bf16[8,16,256]{2,1,0:T(8,128)(2,1)S(1)}, bf16[8,16,256]{2,1,0:T(8,128)(2,1)}, u32[]{:S(2)}) copy-start(bf16[8,16,256]{2,1,0:T(8,128)(2,1)} %param.18) | copy-start | bytes 196612
  0.6 30.4 %copy-start.5 = (s32[2,4]{1,0:T(2,128)S(1)}, s32[2,4]{1,0:T(2,128)}, u32[]{:S(2)}) copy-start(s32[2,4]{1,0:T(2,128)} %param.20) | copy-start | bytes 100
  0.7 31.8 %copy-start.6 = (s32[2]{0:T(128)S(1)}, s32[2]{0:T(128)}, u32[]{:S(2)}) copy-start(s32[2]{0:T(128)} %param.21) | copy-start | bytes 28
  0.7 32.2 %copy-start.1 = (bf16[1,128,256]{2,1,0:T(8,128)(2,1)S(1)}, bf16[1,128,256]{2,1,0:T(8,128)(2,1)}, u32[]{:S(2)}) copy-start(bf16[1,128,256]{2,1,0:T(8,128)(2,1)} %param.16) | copy-start | bytes 196612
  0.7 40.6 %copy-start.2 = (bf16[8,16,256]{2,1,0:T(8,128)(2,1)S(1)}, bf16[8,16,256]{2,1,0:T(8,128)(2,1)}, u32[]{:S(2)}) copy-start(bf16[8,16,256]{2,1,0:T(8,128)(2,1)} %param.19) | copy-start | bytes 196612
  1.5 54.6 %copy-start.3 = (f32[2,3,256]{2,0,1:T(2,128)S(1)}, f32[2,3,256]{2,0,1:T(2,128)}, u32[]{:S(2)}) copy-start(f32[2,3,256]{2,0,1:T(2,128)} %param.23) | copy-start | bytes 18436
  1.5 54.6 %copy-start.4 = (f32[2,3,256]{2,0,1:T(2,128)S(1)}, f32[2,3,256]{2,0,1:T(2,128)}, u32[]{:S(2)}) copy-start(f32[2,3,256]{2,0,1:T(2,128)} %param.24) | copy-start | bytes 18436
  6.0 76.9 %all-to-all-start.1 = ((bf16[128,4,4,128]{3,0,2,1:T(8,128)(2,1)}), bf16[128,4,4,128]{3,0,2,1:T(8,128)(2,1)S(1)}, u32[]{:S(2)}, u32[]{:S(2)}) async-start(bf16[128,4,4,128]{3,0,2,1:T(8,128)(2,1)} %copy.101), calls=%async_computation.1 | async-start | bytes 1048576 | tf_op jit(solution)/shard_map/all_to_all | solution.py:112
  83.8 16.1 %all-to-all-start = ((bf16[128,4,4,128]{3,0,2,1:T(8,128)(2,1)}), bf16[128,4,4,128]{3,0,2,1:T(8,128)(2,1)S(1)}, u32[]{:S(2)}, u32[]{:S(2)}) async-start(bf16[128,4,4,128]{3,0,2,1:T(8,128)(2,1)} %broadcast_in_dim.113), calls=%async_computation | async-start | bytes 1048576 | tf_op jit(solution)/shard_map/all_to_all | solution.py:113
  100.8 18.3 %all-to-all-start.2 = ((bf16[128,4,4,128]{3,0,2,1:T(8,128)(2,1)}), bf16[128,4,4,128]{3,0,2,1:T(8,128)(2,1)S(1)}, u32[]{:S(2)}, u32[]{:S(2)}) async-start(bf16[128,4,4,128]{3,0,2,1:T(8,128)(2,1)} %broadcast_in_dim.118), calls=%async_computation.2 | async-start | bytes 1048576 | tf_op jit(solution)/shard_map/all_to_all | solution.py:114
  123.6 16.1 %all-to-all-start.3 = ((bf16[512,1,4,128]{3,2,1,0:T(4,128)(2,1)}), bf16[512,1,4,128]{3,2,1,0:T(4,128)(2,1)S(1)}, u32[]{:S(2)}, u32[]{:S(2)}) async-start(bf16[512,1,4,128]{3,2,1,0:T(4,128)(2,1)} %copy.106), calls=%async_computation.3 | async-start | bytes 1048576 | tf_op jit(solution)/shard_map/all_to_all | solution.py:122
where the time goes:
time: 144 us; the launch traced here: 141 us
  blocking collectives  69.9 us (49%)
  waiting for transfers between devices  22.2 us (15%)
  starting transfers between devices  21.8 us (15%)
  local copies, waits for them, and re-layouts  12.5 us (9%)
  matrix products  10.2 us (7%)
  other arithmetic  2.84 us (2%)
  between operations  1.64 us (1%)
    all_gather x3, blocking collectives, merged(): everything = jax.tree.map(lambda part: lax.all_gather(part, axis), value)  40.2 us
    all_to_all x1, waiting for transfers between devices, local(): lax.all_to_all(wide_v, 'seq', split_axis=1, concat_axis=0, tiled=True)  11.6 us
    all_to_all x1, waiting for transfers between devices, local(): lax.all_to_all(wide_k, 'seq', split_axis=1, concat_axis=0, tiled=True)  10.6 us
    all_gather x1, blocking collectives, local(): piece_k = lax.all_gather(own_k, 'batch', axis=0, tiled=True)  9.87 us
    all_gather x1, blocking collectives, local(): piece_v = lax.all_gather(own_v, 'batch', axis=0, tiled=True)  8.29 us
    unnamed x1, blocking collectives  8.03 us
    all_to_all x1, starting transfers between devices, local(): lax.all_to_all(wide_v, 'seq', split_axis=1, concat_axis=0, tiled=True)  5.81 us
    all_to_all x1, starting transfers between devices, local(): lax.all_to_all(by_head, 'seq', split_axis=0, concat_axis=1, tiled=True)  5.77 us
  transfers between devices with their start and end apart: 4, of which 2 were waited for; matrix products, arithmetic and copies ran while one was open for 9% of the time, Pallas kernels for 0%

commit v1 on v0

v1 whole, which is shorter than its diff:
```python
import functools

import jax
import jax.numpy as jnp
from jax import lax
from jax.experimental import pallas as pl
from jax.experimental.pallas import tpu as pltpu
from jax.sharding import PartitionSpec as P

HD = 128
MOST = 4
ROWS = 8
LANES = 128
floor_score = -1e30


def halves(x):
    high = x.astype(jnp.bfloat16)
    low = (x - high.astype(jnp.float32)).astype(jnp.bfloat16)
    return high, low


def nt_dot(a, b):
    return lax.dot_general(a, b, (((1,), (1,)), ((), ())), preferred_element_type=jnp.float32)


def tn_dot(a, b):
    return lax.dot_general(a, b, (((0,), (0,)), ((), ())), preferred_element_type=jnp.float32)


def iota(shape, axis):
    return lax.broadcasted_iota(jnp.int32, shape, axis)


def kernel(
    n, nb, page_rows, w_chunks,
    own_ref, tab_ref, len_ref, k_ref, v_ref, ck_ref, cv_ref, dq_ref, dk_ref, dv_ref, q_hbm, w_hbm,
    out_ref, dec_ref,
    kv, q_vm, w_vm, page_send, page_recv, count_send, count_recv, acc_all, stat_all,
    q8, dk8, dv8, y_send, y_recv,
    local_sem, ring_send, ring_recv, page_ss, page_rs, count_ss, count_rs,
    acc_ss, acc_rs, stat_ss, stat_rs, y_ss, y_rs,
):
    me = lax.axis_index("seq")
    mb = lax.axis_index("batch")
    mt = lax.axis_index("tp")
    tok = k_ref.shape[1]
    kw = k_ref.shape[2]
    k_heads = kw // HD
    q_heads = q_vm.shape[1] // HD
    group = q_heads // k_heads
    new, requests, _ = dq_ref.shape
    pages = tok // page_rows
    slots = tab_ref.shape[1]
    pool = ck_ref.shape[0]
    scaling = HD ** (-0.5)
    other = 1 - mt

    q_copy = pltpu.make_async_copy(q_hbm.at[0], q_vm, local_sem.at[0])
    w_copy = pltpu.make_async_copy(w_hbm, w_vm, local_sem.at[1])
    q_copy.start()
    w_copy.start()

    barrier = pltpu.get_barrier_semaphore()
    for k in range(1, n):
        pl.semaphore_signal(barrier, inc=1, device_id={"seq": lax.rem(me + k, n)}, device_id_type=pl.DeviceIdType.MESH)
    for k in range(1, nb):
        pl.semaphore_signal(barrier, inc=1, device_id={"batch": lax.rem(mb + k, nb)}, device_id_type=pl.DeviceIdType.MESH)
    pl.semaphore_signal(barrier, inc=1, device_id={"tp": other}, device_id_type=pl.DeviceIdType.MESH)

    kv[me, :, 0:kw] = k_ref[0]
    kv[me, :, kw:2 * kw] = v_ref[0]

    owners = [own_ref[0, 0, j] for j in range(pages)]
    ranks = []
    for j in range(pages):
        rank = jnp.int32(0)
        for i in range(j):
            rank = rank + jnp.where(owners[i] == owners[j], 1, 0)
        ranks.append(rank)
    wide = MOST * page_rows
    source_page = iota((1, tok), 1) // page_rows
    place = jnp.zeros((1, tok), jnp.int32)
    for j in range(pages):
        place = jnp.where(source_page == j, owners[j] * MOST + ranks[j], place)
    row = iota((nb * wide, tok), 0)
    column = iota((nb * wide, tok), 1)
    chosen = (row // page_rows == place) & (row % page_rows == column % page_rows)
    chosen = jnp.where(chosen, 1.0, 0.0).astype(jnp.bfloat16)
    for half, ref in enumerate((k_ref, v_ref)):
        moved = jnp.dot(chosen, ref[0], preferred_element_type=jnp.float32)
        page_send[:, :, half * kw:(half + 1) * kw] = moved.astype(jnp.bfloat16).reshape(nb, wide, kw)
    for o in range(nb):
        count = jnp.int32(0)
        for j in range(pages):
            count = count + jnp.where(owners[j] == o, 1, 0)
        count_send[o] = jnp.full((ROWS, LANES), count, jnp.int32)
    page_recv[mb] = page_send[mb]
    count_recv[mb] = count_send[mb]

    pl.semaphore_wait(barrier, (n - 1) + (nb - 1) + 1)

    def ring(i):
        block = me - i
        return pltpu.make_async_remote_copy(
            src_ref=kv.at[block], dst_ref=kv.at[block], send_sem=ring_send.at[i], recv_sem=ring_recv.at[i],
            device_id={"seq": me + 1}, device_id_type=pl.DeviceIdType.MESH)

    def arrival(i):
        block = me - 1 - i
        return pltpu.make_async_remote_copy(
            src_ref=kv.at[block], dst_ref=kv.at[block], send_sem=ring_send.at[i], recv_sem=ring_recv.at[i],
            device_id={"seq": me - 1}, device_id_type=pl.DeviceIdType.MESH)

    def page_pair(k):
        to = lax.rem(mb + k, nb)
        return (
            pltpu.make_async_remote_copy(
                src_ref=count_send.at[to], dst_ref=count_recv.at[mb], send_sem=count_ss.at[k - 1],
                recv_sem=count_rs.at[k - 1], device_id={"batch": to}, device_id_type=pl.DeviceIdType.MESH),
            pltpu.make_async_remote_copy(
                src_ref=page_send.at[to], dst_ref=page_recv.at[mb], send_sem=page_ss.at[k - 1],
                recv_sem=page_rs.at[k - 1], device_id={"batch": to}, device_id_type=pl.DeviceIdType.MESH),
        )

    def page_arrival(k):
        since = lax.rem(mb - k + nb, nb)
        return (
            pltpu.make_async_remote_copy(
                src_ref=count_send.at[since], dst_ref=count_recv.at[since], send_sem=count_ss.at[k - 1],
                recv_sem=count_rs.at[k - 1], device_id={"batch": since}, device_id_type=pl.DeviceIdType.MESH),
            pltpu.make_async_remote_copy(
                src_ref=page_send.at[since], dst_ref=page_recv.at[since], send_sem=page_ss.at[k - 1],
                recv_sem=page_rs.at[k - 1], device_id={"batch": since}, device_id_type=pl.DeviceIdType.MESH),
        )

    @pl.when(me < n - 1)
    def _():
        ring(0).start()

    for k in range(1, nb):
        for copy in page_pair(k):
            copy.start()

    def relay(i):
        @pl.when(me > i)
        def _():
            arrival(i).wait_recv()

            @pl.when(me < n - 1)
            def _():
                ring(i + 1).start()

    for j in range(1, n):
        @pl.when(j > me)
        def _():
            kv[j] = jnp.zeros_like(kv[j])

    for packed, ref in ((q8, dq_ref), (dk8, dk_ref), (dv8, dv_ref)):
        packed[...] = jnp.zeros_like(packed)
        for m in range(new):
            packed[m * requests:(m + 1) * requests, :] = ref[m]
    per_head = group * ROWS
    diagonal = []
    for a in range(k_heads):
        rows = jnp.concatenate(
            [q8[:, (a * group + g) * HD:(a * group + g + 1) * HD] for g in range(group)], axis=0)
        nothing = jnp.zeros((per_head, HD), jnp.float32)
        diagonal.append(jnp.concatenate([rows if b == a else nothing for b in range(k_heads)], axis=1))
    dec_q = jnp.concatenate(halves(jnp.concatenate(diagonal, axis=0)), axis=0)
    lanes = k_heads * per_head

    def dec_scores(keys):
        both = nt_dot(keys, dec_q)
        return (both[:, :lanes] + both[:, lanes:]) * scaling

    cache_rows = pool * page_rows
    token = iota((1, lanes), 1) % ROWS
    request = token % requests
    score_cache = dec_scores(ck_ref[...].reshape(cache_rows, kw))
    slot_of = iota((cache_rows, lanes), 0) // page_rows
    within = iota((cache_rows, lanes), 0) % page_rows
    live = jnp.zeros((cache_rows, lanes), jnp.int32)
    for r in range(requests):
        for j in range(slots):
            first = (j * n + me) * page_rows
            named = (slot_of == tab_ref[r, j]) & (request == r) & (first + within < len_ref[r])
            live = jnp.where(named, 1, live)
    score_cache = jnp.where(live > 0, score_cache, floor_score)
    new_k = jnp.concatenate([part.astype(jnp.float32) for part in halves(dk8[...])], axis=0).astype(jnp.bfloat16)
    new_v = jnp.concatenate([part.astype(jnp.float32) for part in halves(dv8[...])], axis=0).astype(jnp.bfloat16)
    score_new = dec_scores(new_k)
    score_new = score_new[:ROWS] + score_new[ROWS:]
    key_token = iota((ROWS, lanes), 0)
    causal = (key_token % requests == request) & (key_token <= token) & (me == 0)
    score_new = jnp.where(causal, score_new, floor_score)

    relay(0)

    for k in range(1, nb):
        for copy in page_arrival(k):
            copy.wait_recv()
    received = page_recv[...].reshape(nb * wide, 2 * kw)
    score_recv = dec_scores(received[:, :kw])
    place_of = iota((wide, lanes), 0) // page_rows
    kept = jnp.concatenate([jnp.where(place_of < count_recv[b][0:1, :], 1, 0) for b in range(nb)], axis=0)
    score_recv = jnp.where(kept > 0, score_recv, floor_score)
    peak = jnp.maximum(
        jnp.maximum(jnp.max(score_cache, axis=0, keepdims=True), jnp.max(score_recv, axis=0, keepdims=True)),
        jnp.max(score_new, axis=0, keepdims=True))
    weight_cache = jnp.where(live > 0, jnp.exp(score_cache - peak), 0.0)
    weight_recv = jnp.where(kept > 0, jnp.exp(score_recv - peak), 0.0)
    weight_new = jnp.where(causal, jnp.exp(score_new - peak), 0.0)
    total = (jnp.sum(weight_cache, axis=0, keepdims=True) + jnp.sum(weight_recv, axis=0, keepdims=True)
             + jnp.sum(weight_new, axis=0, keepdims=True))

    def dec_values(values, weights):
        both = tn_dot(values, jnp.concatenate(halves(weights), axis=1))
        return both[:, :lanes] + both[:, lanes:]

    mixed = dec_values(cv_ref[...].reshape(cache_rows, kw), weight_cache)
    mixed = mixed + dec_values(received[:, kw:], weight_recv)
    mixed = mixed + dec_values(new_v, jnp.concatenate([weight_new, weight_new], axis=0))
    lane_head = iota((HD, lanes), 1) // per_head
    acc = mixed[0:HD]
    for a in range(1, k_heads):
        acc = jnp.where(lane_head == a, mixed[a * HD:(a + 1) * HD], acc)
    acc_all[me] = acc.astype(jnp.bfloat16)
    stat_row = iota((ROWS, lanes), 0)
    stat_all[me] = jnp.where(stat_row == 0, peak, total)

    def partial_pair(k, slot, to):
        return (
            pltpu.make_async_remote_copy(
                src_ref=acc_all.at[slot], dst_ref=acc_all.at[slot], send_sem=acc_ss.at[k - 1],
                recv_sem=acc_rs.at[k - 1], device_id={"seq": to}, device_id_type=pl.DeviceIdType.MESH),
            pltpu.make_async_remote_copy(
                src_ref=stat_all.at[slot], dst_ref=stat_all.at[slot], send_sem=stat_ss.at[k - 1],
                recv_sem=stat_rs.at[k - 1], device_id={"seq": to}, device_id_type=pl.DeviceIdType.MESH),
        )

    for k in range(1, n):
        for copy in partial_pair(k, me, lax.rem(me + k, n)):
            copy.start()

    for i in range(1, n - 2):
        relay(i)

    for k in range(1, n):
        since = lax.rem(me - k + n, n)
        for copy in partial_pair(k, since, since):
            copy.wait_recv()
    peaks = [stat_all[s][0:1, :] for s in range(n)]
    top = functools.reduce(jnp.maximum, peaks)
    scales = [jnp.exp(p - top) for p in peaks]
    whole = sum(stat_all[s][1:2, :] * scales[s] for s in range(n))
    merged = sum(acc_all[s].astype(jnp.float32) * scales[s] for s in range(n)) / whole
    merged = merged.T
    attention = jnp.concatenate([merged[h * ROWS:(h + 1) * ROWS] for h in range(q_heads)], axis=1)
    parts = jnp.concatenate([p.astype(jnp.float32) for p in halves(attention)], axis=0).astype(jnp.bfloat16)
    w_copy.wait()
    step = w_vm.shape[1] // w_chunks

    def y_copy(c):
        return pltpu.make_async_remote_copy(
            src_ref=y_send.at[c], dst_ref=y_recv.at[c], send_sem=y_ss.at[c], recv_sem=y_rs.at[c],
            device_id={"tp": other}, device_id_type=pl.DeviceIdType.MESH)

    for c in range(w_chunks):
        both = jnp.dot(parts, w_vm[:, c * step:(c + 1) * step], preferred_element_type=jnp.float32)
        y_send[c] = both[:ROWS] + both[ROWS:]
        y_copy(c).start()

    q_copy.wait()

    @pl.when(me > n - 2)
    def _():
        arrival(n - 2).wait_recv()

    visible = iota((tok, n * tok), 1) <= iota((tok, n * tok), 0) + me * tok
    at_once = min(4, group)
    for a in range(k_heads):
        def heads(step_id, carry, a=a):
            keys = kv[:, :, a * HD:(a + 1) * HD].reshape(n * tok, HD)
            values = kv[:, :, kw + a * HD:kw + (a + 1) * HD].reshape(n * tok, HD)
            for g in range(at_once):
                start = pl.multiple_of((a * group + step_id * at_once + g) * HD, HD)
                scores = nt_dot(q_vm[:, pl.ds(start, HD)], keys) * scaling
                scores = jnp.where(visible, scores, floor_score)
                weights = jnp.exp(scores - jnp.max(scores, axis=1, keepdims=True))
                sums = jnp.sum(weights, axis=1, keepdims=True)
                mixture = jnp.dot(weights.astype(jnp.bfloat16), values, preferred_element_type=jnp.float32)
                out_ref[0, :, pl.ds(start, HD)] = (mixture / sums).astype(jnp.bfloat16)
            return carry

        lax.fori_loop(0, group // at_once, heads, 0)

    for c in range(w_chunks):
        y_copy(c).wait()
        y = y_send[c] + y_recv[c]
        for m in range(new):
            dec_ref[m, :, c * step:(c + 1) * step] = y[m * requests:(m + 1) * requests]

    for i in range(n - 1):
        @pl.when((me < n - 1) & (me >= i))
        def _():
            ring(i).wait_send()
    for k in range(1, nb):
        for copy in page_pair(k):
            copy.wait_send()
    for k in range(1, n):
        for copy in partial_pair(k, me, lax.rem(me + k, n)):
            copy.wait_send()


def local(
    pre_q, pre_k, pre_v, owner_map, cache_k, cache_v, tables, lengths, dec_q, dec_k, dec_v, w_out
):
    n = lax.axis_size("seq")
    nb = lax.axis_size("batch")
    tok = pre_q.shape[1]
    kw = pre_k.shape[2]
    page_rows = cache_k.shape[1]
    lanes = pre_q.shape[2] // HD * ROWS
    out_columns = w_out.shape[1]
    w_chunks = max(1, out_columns // 512)
    smem = pl.BlockSpec(memory_space=pltpu.SMEM)
    vmem = pl.BlockSpec(memory_space=pltpu.VMEM)
    anywhere = pl.BlockSpec(memory_space=pl.ANY)
    dma = pltpu.SemaphoreType.DMA
    pre_out, dec_out = pl.pallas_call(
        functools.partial(kernel, n, nb, page_rows, w_chunks),
        out_shape=(
            jax.ShapeDtypeStruct(pre_q.shape, jnp.bfloat16),
            jax.ShapeDtypeStruct((dec_q.shape[1], dec_q.shape[0], out_columns), jnp.float32),
        ),
        in_specs=[smem] * 3 + [vmem] * 7 + [anywhere] * 2,
        out_specs=(vmem, vmem),
        scratch_shapes=[
            pltpu.VMEM((n, tok, 2 * kw), jnp.bfloat16),
            pltpu.VMEM((tok, pre_q.shape[2]), jnp.bfloat16),
            pltpu.VMEM(w_out.shape, jnp.bfloat16),
            pltpu.VMEM((nb, MOST * page_rows, 2 * kw), jnp.bfloat16),
            pltpu.VMEM((nb, MOST * page_rows, 2 * kw), jnp.bfloat16),
            pltpu.VMEM((nb, ROWS, LANES), jnp.int32),
            pltpu.VMEM((nb, ROWS, LANES), jnp.int32),
            pltpu.VMEM((n, HD, lanes), jnp.bfloat16),
            pltpu.VMEM((n, ROWS, lanes), jnp.float32),
            pltpu.VMEM((ROWS, dec_q.shape[2]), jnp.float32),
            pltpu.VMEM((ROWS, kw), jnp.float32),
            pltpu.VMEM((ROWS, kw), jnp.float32),
            pltpu.VMEM((w_chunks, ROWS, out_columns // w_chunks), jnp.float32),
            pltpu.VMEM((w_chunks, ROWS, out_columns // w_chunks), jnp.float32),
            dma((2,)),
            dma((n - 1,)), dma((n - 1,)),
            dma((nb - 1,)), dma((nb - 1,)), dma((nb - 1,)), dma((nb - 1,)),
            dma((n - 1,)), dma((n - 1,)), dma((n - 1,)), dma((n - 1,)),
            dma((w_chunks,)), dma((w_chunks,)),
        ],
        compiler_params=pltpu.CompilerParams(
            collective_id=0, has_side_effects=True, vmem_limit_bytes=48 * 1024 * 1024
        ),
        name="prefill_and_decode",
    )(
        jnp.swapaxes(owner_map, 1, 2), tables, lengths, pre_k, pre_v, cache_k, cache_v,
        *(jnp.swapaxes(x, 0, 1) for x in (dec_q, dec_k, dec_v)), pre_q, w_out,
    )
    return pre_out, jnp.swapaxes(dec_out, 0, 1)


def solution(mesh):
    placed = (
        P("batch", "seq", "tp"),
        P("batch", "seq", "tp"),
        P("batch", "seq", "tp"),
        P("batch", "seq", None),
        P("batch", "seq", "tp"),
        P("batch", "seq", "tp"),
        P("batch", "seq"),
        P("batch"),
        P("batch", None, "tp"),
        P("batch", None, "tp"),
        P("batch", None, "tp"),
        P("tp", "seq"),
    )
    return jax.shard_map(
        local,
        mesh=mesh,
        in_specs=placed,
        out_specs=(P("batch", "seq", "tp"), P("batch", None, "seq")),
        check_vma=False,
    )
```

time: 144 us -> 33.1 us (0.23); the launches traced: 141 us -> 32.6 us
  blocking collectives: 69.9 us -> 0 us
  waiting for transfers between devices: 22.2 us -> 0 us
  Pallas kernels: 0 us -> 22 us
  starting transfers between devices: 21.8 us -> 0 us
  matrix products: 10.2 us -> 0 us
  other arithmetic: 2.84 us -> 0 us
  local copies, waits for them, and re-layouts: 12.5 us -> 9.97 us
    all_gather x5 -> x0, blocking collectives: 58.3 us -> none  [the longest x3 40.2 us: merged(): everything = jax.tree.map(lambda part: lax.all_gather(part, axis), value)]
    all_to_all x4 -> x0, waiting for transfers between devices: 22.2 us -> none  [the longest x1 11.6 us: local(): lax.all_to_all(wide_v, 'seq', split_axis=1, concat_axis=0, tiled=True)]
    pallas_call x0 -> x1, Pallas kernels: none -> 22 us  [local(): pl.pallas_call(functools.partial(kernel, n, nb, page_rows, w_chunks), out...]
    all_to_all x4 -> x0, starting transfers between devices: 21.8 us -> none  [the longest x1 5.81 us: local(): lax.all_to_all(wide_v, 'seq', split_axis=1, concat_axis=0, tiled=True)]
    dot_general x9 -> x0, matrix products: 10.2 us -> none  [the longest x1 5.66 us: local(): projected = jnp.dot(attention, w_out.astype(jnp.float32), precision=highest)]
    unnamed x1 -> x0, blocking collectives: 8.03 us -> none
    unnamed x19 -> x24, local copies, waits for them, and re-layouts: 3.51 us -> 9.97 us
    psum x1 -> x0, blocking collectives: 3.59 us -> none  [local(): lax.psum(projected, 'tp').reshape(requests, new_count, projected.shape[1])]
  transfers between devices with their start and end apart: 4 -> 0, of which waited for: 2 -> 0; matrix products, arithmetic and copies ran while one was open for 9% -> 0% of each run, Pallas kernels for 0% -> 0%
where the time goes in v1:
time: 33.1 us; the launch traced here: 32.6 us
  Pallas kernels  22 us (66%)
  local copies, waits for them, and re-layouts  9.97 us (30%)
  between operations  0.66 us (2%)
    pallas_call x1, Pallas kernels, local(): pl.pallas_call(functools.partial(kernel, n, nb, page_rows, w_chunks), out...  22 us
    unnamed x24, local copies, waits for them, and re-layouts  9.97 us

profile of v1, /device:TPU:26, one launch (start us, length us, event | category | flops | bytes accessed | tf_op | source)
XLA Modules:
  0.0 32.6 jit_solution(15977761420739414038)
XLA Ops:
  0.6 0.0 copy-start
  0.6 1.0 %copy-done = bf16[1,128,2048]{2,1,0:T(8,128)(2,1)S(1)} copy-done((bf16[1,128,2048]{2,1,0:T(8,128)(2,1)S(1)}, bf16[1,128,2048]{2,1,0:T(8,128)(2,1)}, u32[]{:S(2)}) %copy-start) | copy-done | bytes 524312
  1.7 0.0 copy-start.1
  1.7 0.8 %copy-done.1 = bf16[1,128,256]{2,1,0:T(8,128)(2,1)S(1)} copy-done((bf16[1,128,256]{2,1,0:T(8,128)(2,1)S(1)}, bf16[1,128,256]{2,1,0:T(8,128)(2,1)}, u32[]{:S(2)}) %copy-start.1) | copy-done | bytes 65560
  2.5 0.0 copy-start.2
  2.5 0.8 %copy-done.2 = bf16[1,128,256]{2,1,0:T(8,128)(2,1)S(1)} copy-done((bf16[1,128,256]{2,1,0:T(8,128)(2,1)S(1)}, bf16[1,128,256]{2,1,0:T(8,128)(2,1)}, u32[]{:S(2)}) %copy-start.2) | copy-done | bytes 65560
  3.4 0.0 copy-start.3
  3.4 0.8 %copy-done.3 = bf16[8,16,256]{2,1,0:T(8,128)(2,1)S(1)} copy-done((bf16[8,16,256]{2,1,0:T(8,128)(2,1)S(1)}, bf16[8,16,256]{2,1,0:T(8,128)(2,1)}, u32[]{:S(2)}) %copy-start.3) | copy-done | bytes 65560
  4.2 0.0 copy-start.4
  4.2 0.8 %copy-done.4 = bf16[8,16,256]{2,1,0:T(8,128)(2,1)S(1)} copy-done((bf16[8,16,256]{2,1,0:T(8,128)(2,1)S(1)}, bf16[8,16,256]{2,1,0:T(8,128)(2,1)}, u32[]{:S(2)}) %copy-start.4) | copy-done | bytes 65560
  5.0 0.0 copy-start.5
  5.0 0.8 %copy-done.5 = f32[2,3,2048]{2,0,1:T(2,128)S(1)} copy-done((f32[2,3,2048]{2,0,1:T(2,128)S(1)}, f32[2,3,2048]{2,0,1:T(2,128)}, u32[]{:S(2)}) %copy-start.5) | copy-done | bytes 49176
  5.8 0.0 copy-start.6
  5.8 0.7 %copy-done.6 = f32[2,3,256]{2,0,1:T(2,128)S(1)} copy-done((f32[2,3,256]{2,0,1:T(2,128)S(1)}, f32[2,3,256]{2,0,1:T(2,128)}, u32[]{:S(2)}) %copy-start.6) | copy-done | bytes 6168
  6.5 0.0 copy-start.7
  6.5 0.7 %copy-done.7 = f32[2,3,256]{2,0,1:T(2,128)S(1)} copy-done((f32[2,3,256]{2,0,1:T(2,128)S(1)}, f32[2,3,256]{2,0,1:T(2,128)}, u32[]{:S(2)}) %copy-start.7) | copy-done | bytes 6168
  7.2 0.0 copy-start.8
  7.2 0.7 %copy-done.8 = s32[2,4]{1,0:T(2,128)S(1)} copy-done((s32[2,4]{1,0:T(2,128)S(1)}, s32[2,4]{1,0:T(2,128)}, u32[]{:S(2)}) %copy-start.8) | copy-done | bytes 56
  7.9 0.0 copy-start.9
  7.9 0.7 %copy-done.9 = s32[1,8,1]{1,2,0:T(1,128)S(1)} copy-done((s32[1,8,1]{1,2,0:T(1,128)S(1)}, s32[1,8,1]{1,2,0:T(1,128)}, u32[]{:S(2)}) %copy-start.9) | copy-done | bytes 56
  8.6 0.0 copy-start.10
  8.6 0.7 %copy-done.10 = s32[2]{0:T(128)S(1)} copy-done((s32[2]{0:T(128)S(1)}, s32[2]{0:T(128)}, u32[]{:S(2)}) %copy-start.10) | copy-done | bytes 32
  9.2 22.0 %prefill_and_decode.1 = (bf16[1,128,2048]{2,1,0:T(8,128)(2,1)S(1)}, f32[3,2,2048]{2,1,0:T(2,128)S(1)}) custom-call(s32[1,1,8]{2,1,0:T(1,128)S(1)} %bitcast.9, s32[2,4]{1,0:T(2,128)S(1)} %copy-done.8, s32[2]{0:T(128)S(1)} %copy-done.10, bf16[1,128,256]{2,1,0:T(8,128)(2,1)S(1)} %copy-done.1, bf16[1,128,256]{2,1,0:T(8,128)(2,1)S(1)} %copy-done.2, ...), custom_call_target="tpu_custom_call" | custom-call | tf_op jit(solution)/shard_map/prefill_and_decode/pallas_call | solution.py:331
  31.2 0.8 %copy.16 = bf16[1,128,2048]{2,1,0:T(8,128)(2,1)} copy(bf16[1,128,2048]{2,1,0:T(8,128)(2,1)S(1)} %get-tuple-element.8) | data formatting | bytes 1048576
  32.0 0.6 %copy.17 = f32[2,3,2048]{2,0,1:T(2,128)} copy(f32[2,3,2048]{2,0,1:T(2,128)S(1)} %bitcast.6) | data formatting | bytes 98304
Async XLA Ops:
  0.6 1.0 %copy-start = (bf16[1,128,2048]{2,1,0:T(8,128)(2,1)S(1)}, bf16[1,128,2048]{2,1,0:T(8,128)(2,1)}, u32[]{:S(2)}) copy-start(bf16[1,128,2048]{2,1,0:T(8,128)(2,1)} %q_hbm.1) | copy-start | bytes 1572868
  1.7 0.8 %copy-start.1 = (bf16[1,128,256]{2,1,0:T(8,128)(2,1)S(1)}, bf16[1,128,256]{2,1,0:T(8,128)(2,1)}, u32[]{:S(2)}) copy-start(bf16[1,128,256]{2,1,0:T(8,128)(2,1)} %k_ref.1) | copy-start | bytes 196612
  2.5 0.8 %copy-start.2 = (bf16[1,128,256]{2,1,0:T(8,128)(2,1)S(1)}, bf16[1,128,256]{2,1,0:T(8,128)(2,1)}, u32[]{:S(2)}) copy-start(bf16[1,128,256]{2,1,0:T(8,128)(2,1)} %v_ref.1) | copy-start | bytes 196612
  3.4 0.8 %copy-start.3 = (bf16[8,16,256]{2,1,0:T(8,128)(2,1)S(1)}, bf16[8,16,256]{2,1,0:T(8,128)(2,1)}, u32[]{:S(2)}) copy-start(bf16[8,16,256]{2,1,0:T(8,128)(2,1)} %ck_ref.1) | copy-start | bytes 196612
  4.2 0.8 %copy-start.4 = (bf16[8,16,256]{2,1,0:T(8,128)(2,1)S(1)}, bf16[8,16,256]{2,1,0:T(8,128)(2,1)}, u32[]{:S(2)}) copy-start(bf16[8,16,256]{2,1,0:T(8,128)(2,1)} %cv_ref.1) | copy-start | bytes 196612
  5.0 0.8 %copy-start.5 = (f32[2,3,2048]{2,0,1:T(2,128)S(1)}, f32[2,3,2048]{2,0,1:T(2,128)}, u32[]{:S(2)}) copy-start(f32[2,3,2048]{2,0,1:T(2,128)} %param.20) | copy-start | bytes 147460
  5.8 0.7 %copy-start.6 = (f32[2,3,256]{2,0,1:T(2,128)S(1)}, f32[2,3,256]{2,0,1:T(2,128)}, u32[]{:S(2)}) copy-start(f32[2,3,256]{2,0,1:T(2,128)} %param.21) | copy-start | bytes 18436
  6.5 0.7 %copy-start.7 = (f32[2,3,256]{2,0,1:T(2,128)S(1)}, f32[2,3,256]{2,0,1:T(2,128)}, u32[]{:S(2)}) copy-start(f32[2,3,256]{2,0,1:T(2,128)} %param.22) | copy-start | bytes 18436
  7.2 0.7 %copy-start.8 = (s32[2,4]{1,0:T(2,128)S(1)}, s32[2,4]{1,0:T(2,128)}, u32[]{:S(2)}) copy-start(s32[2,4]{1,0:T(2,128)} %tab_ref.1) | copy-start | bytes 100
  7.9 0.7 %copy-start.9 = (s32[1,8,1]{1,2,0:T(1,128)S(1)}, s32[1,8,1]{1,2,0:T(1,128)}, u32[]{:S(2)}) copy-start(s32[1,8,1]{1,2,0:T(1,128)} %param.15) | copy-start | bytes 100
  8.6 0.7 %copy-start.10 = (s32[2]{0:T(128)S(1)}, s32[2]{0:T(128)}, u32[]{:S(2)}) copy-start(s32[2]{0:T(128)} %len_ref.1) | copy-start | bytes 28

commit v2 on v1

--- a/solution.py
+++ b/solution.py
@@ -34,18 +34,19 @@
 
 def kernel(
     n, nb, page_rows, w_chunks,
-    own_ref, tab_ref, len_ref, k_ref, v_ref, ck_ref, cv_ref, dq_ref, dk_ref, dv_ref, q_hbm, w_hbm,
-    out_ref, dec_ref,
+    own_hbm, tab_hbm, len_hbm, k_hbm, v_hbm, ck_hbm, cv_hbm, dq_hbm, dk_hbm, dv_hbm, q_hbm, w_hbm,
+    out_hbm, dec_ref,
+    out_ref, own_ref, tab_ref, len_ref, ck_ref, cv_ref, dq_ref, dk_ref, dv_ref, mix_ref, peak_ref, total_ref,
     kv, q_vm, w_vm, page_send, page_recv, count_send, count_recv, acc_all, stat_all,
     q8, dk8, dv8, y_send, y_recv,
-    local_sem, ring_send, ring_recv, page_ss, page_rs, count_ss, count_rs,
+    local_sem, out_sem, ring_send, ring_recv, page_ss, page_rs, count_ss, count_rs,
     acc_ss, acc_rs, stat_ss, stat_rs, y_ss, y_rs,
 ):
     me = lax.axis_index("seq")
     mb = lax.axis_index("batch")
     mt = lax.axis_index("tp")
-    tok = k_ref.shape[1]
-    kw = k_ref.shape[2]
+    tok = k_hbm.shape[1]
+    kw = k_hbm.shape[2]
     k_heads = kw // HD
     q_heads = q_vm.shape[1] // HD
     group = q_heads // k_heads
@@ -56,11 +57,6 @@
     scaling = HD ** (-0.5)
     other = 1 - mt
 
-    q_copy = pltpu.make_async_copy(q_hbm.at[0], q_vm, local_sem.at[0])
-    w_copy = pltpu.make_async_copy(w_hbm, w_vm, local_sem.at[1])
-    q_copy.start()
-    w_copy.start()
-
     barrier = pltpu.get_barrier_semaphore()
     for k in range(1, n):
         pl.semaphore_signal(barrier, inc=1, device_id={"seq": lax.rem(me + k, n)}, device_id_type=pl.DeviceIdType.MESH)
@@ -68,8 +64,18 @@
         pl.semaphore_signal(barrier, inc=1, device_id={"batch": lax.rem(mb + k, nb)}, device_id_type=pl.DeviceIdType.MESH)
     pl.semaphore_signal(barrier, inc=1, device_id={"tp": other}, device_id_type=pl.DeviceIdType.MESH)
 
-    kv[me, :, 0:kw] = k_ref[0]
-    kv[me, :, kw:2 * kw] = v_ref[0]
+    mine = kv.at[me]
+    sources = (
+        (k_hbm.at[0], mine.at[:, pl.ds(0, kw)]), (v_hbm.at[0], mine.at[:, pl.ds(kw, kw)]), (own_hbm, own_ref),
+        (dq_hbm, dq_ref), (dk_hbm, dk_ref), (dv_hbm, dv_ref), (tab_hbm, tab_ref), (len_hbm, len_ref),
+        (ck_hbm, ck_ref), (cv_hbm, cv_ref), (q_hbm.at[0], q_vm), (w_hbm, w_vm))
+    copies = [pltpu.make_async_copy(a, b, local_sem.at[i]) for i, (a, b) in enumerate(sources)]
+    for copy in copies:
+        copy.start()
+    w_copy = copies.pop()
+    q_copy = copies.pop()
+    for copy in copies[:3]:
+        copy.wait()
 
     owners = [own_ref[0, 0, j] for j in range(pages)]
     ranks = []
@@ -87,9 +93,8 @@
     column = iota((nb * wide, tok), 1)
     chosen = (row // page_rows == place) & (row % page_rows == column % page_rows)
     chosen = jnp.where(chosen, 1.0, 0.0).astype(jnp.bfloat16)
-    for half, ref in enumerate((k_ref, v_ref)):
-        moved = jnp.dot(chosen, ref[0], preferred_element_type=jnp.float32)
-        page_send[:, :, half * kw:(half + 1) * kw] = moved.astype(jnp.bfloat16).reshape(nb, wide, kw)
+    moved = jnp.dot(chosen, kv[me], preferred_element_type=jnp.float32)
+    page_send[...] = moved.astype(jnp.bfloat16).reshape(nb, wide, 2 * kw)
     for o in range(nb):
         count = jnp.int32(0)
         for j in range(pages):
@@ -151,10 +156,8 @@
             def _():
                 ring(i + 1).start()
 
-    for j in range(1, n):
-        @pl.when(j > me)
-        def _():
-            kv[j] = jnp.zeros_like(kv[j])
+    for copy in copies[3:]:
+        copy.wait()
 
     for packed, ref in ((q8, dq_ref), (dk8, dk_ref), (dv8, dv_ref)):
         packed[...] = jnp.zeros_like(packed)
@@ -195,6 +198,38 @@
     causal = (key_token % requests == request) & (key_token <= token) & (me == 0)
     score_new = jnp.where(causal, score_new, floor_score)
 
+    pair = 2
+    pair_lanes = pair * tok
+
+    def prefill_block(block, first):
+        for a in range(k_heads):
+            keys = kv[block, :, a * HD:(a + 1) * HD]
+            values = kv[block, :, kw + a * HD:kw + (a + 1) * HD].T
+            for p in range(group // pair):
+                at = a * (group // pair) + p
+                queries = jnp.concatenate(
+                    [q_vm[:, (at * pair + i) * HD:(at * pair + i + 1) * HD] for i in range(pair)], axis=0)
+                scores = nt_dot(keys, queries) * scaling
+                if first:
+                    visible = iota((tok, pair_lanes), 0) <= iota((tok, pair_lanes), 1) % tok
+                    scores = jnp.where(visible, scores, floor_score)
+                high = jnp.max(scores, axis=0, keepdims=True)
+                if not first:
+                    before = peak_ref[at, 0:1, :]
+                    high = jnp.maximum(high, before)
+                weights = jnp.exp(scores - high)
+                sums = jnp.sum(weights, axis=0, keepdims=True)
+                mixture = jnp.dot(values, weights.astype(jnp.bfloat16), preferred_element_type=jnp.float32)
+                if not first:
+                    shrink = jnp.exp(before - high)
+                    sums = sums + total_ref[at, 0:1, :] * shrink
+                    mixture = mixture + mix_ref[at] * shrink
+                peak_ref[at, 0:1, :] = high
+                total_ref[at, 0:1, :] = sums
+                mix_ref[at] = mixture
+
+    q_copy.wait()
+    prefill_block(me, True)
     relay(0)
 
     for k in range(1, nb):
@@ -243,8 +278,9 @@
         for copy in partial_pair(k, me, lax.rem(me + k, n)):
             copy.start()
 
-    for i in range(1, n - 2):
-        relay(i)
+    @pl.when(me >= 1)
+    def _():
+        prefill_block(me - 1, False)
 
     for k in range(1, n):
         since = lax.rem(me - k + n, n)
@@ -271,29 +307,32 @@
         y_send[c] = both[:ROWS] + both[ROWS:]
         y_copy(c).start()
 
-    q_copy.wait()
-
-    @pl.when(me > n - 2)
-    def _():
-        arrival(n - 2).wait_recv()
-
-    visible = iota((tok, n * tok), 1) <= iota((tok, n * tok), 0) + me * tok
-    at_once = min(4, group)
-    for a in range(k_heads):
-        def heads(step_id, carry, a=a):
-            keys = kv[:, :, a * HD:(a + 1) * HD].reshape(n * tok, HD)
-            values = kv[:, :, kw + a * HD:kw + (a + 1) * HD].reshape(n * tok, HD)
-            for g in range(at_once):
-                start = pl.multiple_of((a * group + step_id * at_once + g) * HD, HD)
-                scores = nt_dot(q_vm[:, pl.ds(start, HD)], keys) * scaling
-                scores = jnp.where(visible, scores, floor_score)
-                weights = jnp.exp(scores - jnp.max(scores, axis=1, keepdims=True))
-                sums = jnp.sum(weights, axis=1, keepdims=True)
-                mixture = jnp.dot(weights.astype(jnp.bfloat16), values, preferred_element_type=jnp.float32)
-                out_ref[0, :, pl.ds(start, HD)] = (mixture / sums).astype(jnp.bfloat16)
-            return carry
-
-        lax.fori_loop(0, group // at_once, heads, 0)
+    def later(i, carry):
+        @pl.when(me >= i)
+        def _():
+            arrival(i - 1).wait_recv()
+
+            @pl.when(me < n - 1)
+            def _():
+                ring(i).start()
+
+            prefill_block(me - i, False)
+        return carry
+
+    lax.fori_loop(2, n, later, 0)
+
+    def out_copy(at):
+        columns = pl.ds(at * pair * HD, pair * HD)
+        return pltpu.make_async_copy(out_ref.at[:, columns], out_hbm.at[0, :, columns], out_sem.at[at])
+
+    unit = jnp.where(iota((tok, tok), 0) == iota((tok, tok), 1), 1.0, 0.0).astype(jnp.bfloat16)
+    for at in range(q_heads // pair):
+        done = (mix_ref[at] / total_ref[at, 0:1, :]).astype(jnp.bfloat16)
+        for i in range(pair):
+            turned = nt_dot(unit, done[:, i * tok:(i + 1) * tok])
+            head = at * pair + i
+            out_ref[:, head * HD:(head + 1) * HD] = turned.astype(jnp.bfloat16)
+        out_copy(at).start()
 
     for c in range(w_chunks):
         y_copy(c).wait()
@@ -301,6 +340,8 @@
         for m in range(new):
             dec_ref[m, :, c * step:(c + 1) * step] = y[m * requests:(m + 1) * requests]
 
+    for at in range(q_heads // pair):
+        out_copy(at).wait()
     for i in range(n - 1):
         @pl.when((me < n - 1) & (me >= i))
         def _():
@@ -324,9 +365,8 @@
     lanes = pre_q.shape[2] // HD * ROWS
     out_columns = w_out.shape[1]
     w_chunks = max(1, out_columns // 512)
-    smem = pl.BlockSpec(memory_space=pltpu.SMEM)
     vmem = pl.BlockSpec(memory_space=pltpu.VMEM)
-    anywhere = pl.BlockSpec(memory_space=pl.ANY)
+    hbm = pl.BlockSpec(memory_space=pltpu.HBM)
     dma = pltpu.SemaphoreType.DMA
     pre_out, dec_out = pl.pallas_call(
         functools.partial(kernel, n, nb, page_rows, w_chunks),
@@ -334,9 +374,21 @@
             jax.ShapeDtypeStruct(pre_q.shape, jnp.bfloat16),
             jax.ShapeDtypeStruct((dec_q.shape[1], dec_q.shape[0], out_columns), jnp.float32),
         ),
-        in_specs=[smem] * 3 + [vmem] * 7 + [anywhere] * 2,
-        out_specs=(vmem, vmem),
+        in_specs=[hbm] * 12,
+        out_specs=(hbm, vmem),
         scratch_shapes=[
+            pltpu.VMEM(pre_q.shape[1:], jnp.bfloat16),
+            pltpu.SMEM((1, 1, owner_map.shape[1]), jnp.int32),
+            pltpu.SMEM(tables.shape, jnp.int32),
+            pltpu.SMEM(lengths.shape, jnp.int32),
+            pltpu.VMEM(cache_k.shape, jnp.bfloat16),
+            pltpu.VMEM(cache_v.shape, jnp.bfloat16),
+            pltpu.VMEM((dec_q.shape[1], dec_q.shape[0], dec_q.shape[2]), jnp.float32),
+            pltpu.VMEM((dec_q.shape[1], dec_q.shape[0], kw), jnp.float32),
+            pltpu.VMEM((dec_q.shape[1], dec_q.shape[0], kw), jnp.float32),
+            pltpu.VMEM((lanes // (2 * ROWS), HD, 2 * tok), jnp.float32),
+            pltpu.VMEM((lanes // (2 * ROWS), ROWS, 2 * tok), jnp.float32),
+            pltpu.VMEM((lanes // (2 * ROWS), ROWS, 2 * tok), jnp.float32),
             pltpu.VMEM((n, tok, 2 * kw), jnp.bfloat16),
             pltpu.VMEM((tok, pre_q.shape[2]), jnp.bfloat16),
             pltpu.VMEM(w_out.shape, jnp.bfloat16),
@@ -351,14 +403,14 @@
             pltpu.VMEM((ROWS, kw), jnp.float32),
             pltpu.VMEM((w_chunks, ROWS, out_columns // w_chunks), jnp.float32),
             pltpu.VMEM((w_chunks, ROWS, out_columns // w_chunks), jnp.float32),
-            dma((2,)),
+            dma((12,)), dma((lanes // (2 * ROWS),)),
             dma((n - 1,)), dma((n - 1,)),
             dma((nb - 1,)), dma((nb - 1,)), dma((nb - 1,)), dma((nb - 1,)),
             dma((n - 1,)), dma((n - 1,)), dma((n - 1,)), dma((n - 1,)),
             dma((w_chunks,)), dma((w_chunks,)),
         ],
         compiler_params=pltpu.CompilerParams(
-            collective_id=0, has_side_effects=True, vmem_limit_bytes=48 * 1024 * 1024
+            collective_id=0, has_side_effects=True, vmem_limit_bytes=60 * 1024 * 1024
         ),
         name="prefill_and_decode",
     )(

time: 33.1 us -> 25.5 us (0.77)
  local copies, waits for them, and re-layouts: 9.97 us -> 3.3 us
  Pallas kernels: 22 us -> 21.4 us
    unnamed x24 -> x2, local copies, waits for them, and re-layouts: 9.97 us -> 3.3 us
    pallas_call x1, Pallas kernels: 22 us -> 21.4 us  [local(): pl.pallas_call(functools.partial(kernel, n, nb, page_rows, w_chunks), out...]
where the time goes in v2:
time: 25.5 us; the launch traced here: 25.3 us
  Pallas kernels  21.4 us (84%)
  local copies, waits for them, and re-layouts  3.3 us (13%)
  between operations  0.64 us (3%)
    pallas_call x1, Pallas kernels, local(): pl.pallas_call(functools.partial(kernel, n, nb, page_rows, w_chunks), out...  21.4 us
    unnamed x2, local copies, waits for them, and re-layouts  3.3 us

profile of v2, /device:TPU:26, one launch (start us, length us, event | category | flops | bytes accessed | tf_op | source)
XLA Modules:
  0.0 25.3 jit_solution(14968103405261549633)
XLA Ops:
  0.6 21.4 %prefill_and_decode.1 = (bf16[1,128,2048]{2,1,0:T(8,128)(2,1)}, f32[3,2,2048]{2,1,0:T(2,128)}) custom-call(s32[1,1,8]{2,1,0:T(1,128)} %bitcast.9, s32[2,4]{1,0:T(2,128)} %tab_hbm.1, s32[2]{0:T(128)} %len_hbm.1, bf16[1,128,256]{2,1,0:T(8,128)(2,1)} %k_hbm.1, bf16[1,128,256]{2,1,0:T(8,128)(2,1)} %v_hbm.1, bf16[8,16,256]{2,1,0:T(8,128)(2,1)} %ck_hbm.1, ...), custom_call_target="tpu_custom_call" | custom-call | tf_op jit(solution)/shard_map/prefill_and_decode/pallas_call | solution.py:371
  22.0 1.9 %copy.16 = bf16[1,128,2048]{2,1,0:T(8,128)(2,1)} copy(bf16[1,128,2048]{2,1,0:T(8,128)(2,1)} %get-tuple-element.8) | data formatting | bytes 1048576
  23.9 1.4 %copy.17 = f32[2,3,2048]{2,0,1:T(2,128)} copy(f32[2,3,2048]{2,0,1:T(2,128)} %bitcast.6) | data formatting | bytes 98304

commit v3 on v2

--- a/solution.py
+++ b/solution.py
@@ -35,11 +35,11 @@
 def kernel(
     n, nb, page_rows, w_chunks,
     own_hbm, tab_hbm, len_hbm, k_hbm, v_hbm, ck_hbm, cv_hbm, dq_hbm, dk_hbm, dv_hbm, q_hbm, w_hbm,
-    out_hbm, dec_ref,
-    out_ref, own_ref, tab_ref, len_ref, ck_ref, cv_ref, dq_ref, dk_ref, dv_ref, mix_ref, peak_ref, total_ref,
+    out_ref, dec_ref,
+    own_ref, tab_ref, len_ref, ck_ref, cv_ref, dq_ref, dk_ref, dv_ref, mix_ref, peak_ref, total_ref,
     kv, q_vm, w_vm, page_send, page_recv, count_send, count_recv, acc_all, stat_all,
     q8, dk8, dv8, y_send, y_recv,
-    local_sem, out_sem, ring_send, ring_recv, page_ss, page_rs, count_ss, count_rs,
+    local_sem, ring_send, ring_recv, page_ss, page_rs, count_ss, count_rs,
     acc_ss, acc_rs, stat_ss, stat_rs, y_ss, y_rs,
 ):
     me = lax.axis_index("seq")
@@ -282,6 +282,9 @@
     def _():
         prefill_block(me - 1, False)
 
+    if n > 2:
+        relay(1)
+
     for k in range(1, n):
         since = lax.rem(me - k + n, n)
         for copy in partial_pair(k, since, since):
@@ -308,7 +311,7 @@
         y_copy(c).start()
 
     def later(i, carry):
-        @pl.when(me >= i)
+        @pl.when((me >= i) & (i > 2))
         def _():
             arrival(i - 1).wait_recv()
 
@@ -316,14 +319,12 @@
             def _():
                 ring(i).start()
 
+        @pl.when(me >= i)
+        def _():
             prefill_block(me - i, False)
         return carry
 
     lax.fori_loop(2, n, later, 0)
-
-    def out_copy(at):
-        columns = pl.ds(at * pair * HD, pair * HD)
-        return pltpu.make_async_copy(out_ref.at[:, columns], out_hbm.at[0, :, columns], out_sem.at[at])
 
     unit = jnp.where(iota((tok, tok), 0) == iota((tok, tok), 1), 1.0, 0.0).astype(jnp.bfloat16)
     for at in range(q_heads // pair):
@@ -331,8 +332,7 @@
         for i in range(pair):
             turned = nt_dot(unit, done[:, i * tok:(i + 1) * tok])
             head = at * pair + i
-            out_ref[:, head * HD:(head + 1) * HD] = turned.astype(jnp.bfloat16)
-        out_copy(at).start()
+            out_ref[0, :, head * HD:(head + 1) * HD] = turned.astype(jnp.bfloat16)
 
     for c in range(w_chunks):
         y_copy(c).wait()
@@ -340,8 +340,6 @@
         for m in range(new):
             dec_ref[m, :, c * step:(c + 1) * step] = y[m * requests:(m + 1) * requests]
 
-    for at in range(q_heads // pair):
-        out_copy(at).wait()
     for i in range(n - 1):
         @pl.when((me < n - 1) & (me >= i))
         def _():
@@ -352,6 +350,15 @@
     for k in range(1, n):
         for copy in partial_pair(k, me, lax.rem(me + k, n)):
             copy.wait_send()
+
+
+def hand_over(pre_ref, dec_ref, pre_hbm, dec_hbm, sems):
+    copies = [
+        pltpu.make_async_copy(a, b, sems.at[i]) for i, (a, b) in enumerate(((pre_ref, pre_hbm), (dec_ref, dec_hbm)))]
+    for copy in copies:
+        copy.start()
+    for copy in copies:
+        copy.wait()
 
 
 def local(
@@ -371,13 +378,12 @@
     pre_out, dec_out = pl.pallas_call(
         functools.partial(kernel, n, nb, page_rows, w_chunks),
         out_shape=(
-            jax.ShapeDtypeStruct(pre_q.shape, jnp.bfloat16),
-            jax.ShapeDtypeStruct((dec_q.shape[1], dec_q.shape[0], out_columns), jnp.float32),
+            pltpu.VMEM(pre_q.shape, jnp.bfloat16),
+            pltpu.VMEM((dec_q.shape[1], dec_q.shape[0], out_columns), jnp.float32),
         ),
         in_specs=[hbm] * 12,
-        out_specs=(hbm, vmem),
+        out_specs=(vmem, vmem),
         scratch_shapes=[
-            pltpu.VMEM(pre_q.shape[1:], jnp.bfloat16),
             pltpu.SMEM((1, 1, owner_map.shape[1]), jnp.int32),
             pltpu.SMEM(tables.shape, jnp.int32),
             pltpu.SMEM(lengths.shape, jnp.int32),
@@ -403,20 +409,28 @@
             pltpu.VMEM((ROWS, kw), jnp.float32),
             pltpu.VMEM((w_chunks, ROWS, out_columns // w_chunks), jnp.float32),
             pltpu.VMEM((w_chunks, ROWS, out_columns // w_chunks), jnp.float32),
-            dma((12,)), dma((lanes // (2 * ROWS),)),
+            dma((12,)),
             dma((n - 1,)), dma((n - 1,)),
             dma((nb - 1,)), dma((nb - 1,)), dma((nb - 1,)), dma((nb - 1,)),
             dma((n - 1,)), dma((n - 1,)), dma((n - 1,)), dma((n - 1,)),
             dma((w_chunks,)), dma((w_chunks,)),
         ],
         compiler_params=pltpu.CompilerParams(
-            collective_id=0, has_side_effects=True, vmem_limit_bytes=60 * 1024 * 1024
+            collective_id=0, has_side_effects=True, vmem_limit_bytes=48 * 1024 * 1024
         ),
         name="prefill_and_decode",
-    )(
+    )(*(pltpu.with_memory_space_constraint(x, pltpu.HBM) for x in (
         jnp.swapaxes(owner_map, 1, 2), tables, lengths, pre_k, pre_v, cache_k, cache_v,
         *(jnp.swapaxes(x, 0, 1) for x in (dec_q, dec_k, dec_v)), pre_q, w_out,
-    )
+    )))
+    pre_out, dec_out = pl.pallas_call(
+        hand_over,
+        out_shape=(pltpu.HBM(pre_out.shape, pre_out.dtype), pltpu.HBM(dec_out.shape, dec_out.dtype)),
+        in_specs=[vmem] * 2,
+        out_specs=(hbm, hbm),
+        scratch_shapes=[dma((2,))],
+        name="hand_over",
+    )(*(pltpu.with_memory_space_constraint(x, pltpu.VMEM) for x in (pre_out, dec_out)))
     return pre_out, jnp.swapaxes(dec_out, 0, 1)
 
 

time: 25.5 us -> 19.6 us (0.77)
  local copies, waits for them, and re-layouts: 3.3 us -> 0 us
  Pallas kernels: 21.4 us -> 18.8 us
    pallas_call x1, Pallas kernels: 21.4 us -> 18 us  [local(): pl.pallas_call(functools.partial(kernel, n, nb, page_rows, w_chunks), out...]
    unnamed x2 -> x0, local copies, waits for them, and re-layouts: 3.3 us -> none
    pallas_call x0 -> x1, Pallas kernels: none -> 0.81 us  [local(): pl.pallas_call(hand_over, out_shape=(pltpu.HBM(pre_out.shape, pre_out.dty...]
where the time goes in v3:
time: 19.6 us; the launch traced here: 19.4 us
  Pallas kernels  18.8 us (96%)
  between operations  0.64 us (3%)
    pallas_call x1, Pallas kernels, local(): pl.pallas_call(functools.partial(kernel, n, nb, page_rows, w_chunks), out...  18 us
    pallas_call x1, Pallas kernels, local(): pl.pallas_call(hand_over, out_shape=(pltpu.HBM(pre_out.shape, pre_out.dty...  0.81 us

profile of v3, /device:TPU:26, one launch (start us, length us, event | category | flops | bytes accessed | tf_op | source)
XLA Modules:
  0.0 19.4 jit_solution(6799184965504420576)
XLA Ops:
  0.6 18.0 %prefill_and_decode.1 = (bf16[1,128,2048]{2,1,0:T(8,128)(2,1)S(1)}, f32[3,2,2048]{2,1,0:T(2,128)S(1)}) custom-call(s32[1,1,8]{2,1,0:T(1,128)} %bitcast.8, s32[2,4]{1,0:T(2,128)} %tab_hbm.1, s32[2]{0:T(128)} %len_hbm.1, bf16[1,128,256]{2,1,0:T(8,128)(2,1)} %k_hbm.1, bf16[1,128,256]{2,1,0:T(8,128)(2,1)} %v_hbm.1, bf16[8,16,256]{2,1,0:T(8,128)(2,1)} %ck_hbm.1, ...), custom_call_target="tpu_custom_call" | custom-call | tf_op jit(solution)/shard_map/prefill_and_decode/pallas_call | solution.py:378
  18.6 0.8 %hand_over.1 = (bf16[1,128,2048]{2,1,0:T(8,128)(2,1)}, f32[3,2,2048]{2,1,0:T(2,128)}) custom-call(bf16[1,128,2048]{2,1,0:T(8,128)(2,1)S(1)} %get-tuple-element.6.pre_ref, f32[3,2,2048]{2,1,0:T(2,128)S(1)} %get-tuple-element.7.dec_ref), custom_call_target="tpu_custom_call" | custom-call | tf_op jit(solution)/shard_map/hand_over/pallas_call | solution.py:426

commit v4 on v3

--- a/solution.py
+++ b/solution.py
@@ -12,6 +12,7 @@
 ROWS = 8
 LANES = 128
 floor_score = -1e30
+LOG2E = 1.4426950408889634
 
 
 def halves(x):
@@ -148,13 +149,15 @@
             copy.start()
 
     def relay(i):
-        @pl.when(me > i)
+        @pl.when((me > i) & (me < n - 1))
         def _():
             arrival(i).wait_recv()
-
-            @pl.when(me < n - 1)
-            def _():
-                ring(i + 1).start()
+            ring(i + 1).start()
+
+    def last_arrival(i):
+        @pl.when(me == n - 1)
+        def _():
+            arrival(i).wait_recv()
 
     for copy in copies[3:]:
         copy.wait()
@@ -200,6 +203,8 @@
 
     pair = 2
     pair_lanes = pair * tok
+    sharpness = scaling * LOG2E
+    visible = iota((tok, pair_lanes), 0) <= iota((tok, pair_lanes), 1) % tok
 
     def prefill_block(block, first):
         for a in range(k_heads):
@@ -209,19 +214,18 @@
                 at = a * (group // pair) + p
                 queries = jnp.concatenate(
                     [q_vm[:, (at * pair + i) * HD:(at * pair + i + 1) * HD] for i in range(pair)], axis=0)
-                scores = nt_dot(keys, queries) * scaling
+                scores = nt_dot(keys, queries)
                 if first:
-                    visible = iota((tok, pair_lanes), 0) <= iota((tok, pair_lanes), 1) % tok
                     scores = jnp.where(visible, scores, floor_score)
                 high = jnp.max(scores, axis=0, keepdims=True)
                 if not first:
                     before = peak_ref[at, 0:1, :]
                     high = jnp.maximum(high, before)
-                weights = jnp.exp(scores - high)
+                weights = jnp.exp2((scores - high) * sharpness)
                 sums = jnp.sum(weights, axis=0, keepdims=True)
                 mixture = jnp.dot(values, weights.astype(jnp.bfloat16), preferred_element_type=jnp.float32)
                 if not first:
-                    shrink = jnp.exp(before - high)
+                    shrink = jnp.exp2((before - high) * sharpness)
                     sums = sums + total_ref[at, 0:1, :] * shrink
                     mixture = mixture + mix_ref[at] * shrink
                 peak_ref[at, 0:1, :] = high
@@ -278,12 +282,19 @@
         for copy in partial_pair(k, me, lax.rem(me + k, n)):
             copy.start()
 
+    last_arrival(0)
+
     @pl.when(me >= 1)
     def _():
         prefill_block(me - 1, False)
 
     if n > 2:
         relay(1)
+        last_arrival(1)
+
+        @pl.when(me >= 2)
+        def _():
+            prefill_block(me - 2, False)
 
     for k in range(1, n):
         since = lax.rem(me - k + n, n)
@@ -311,7 +322,7 @@
         y_copy(c).start()
 
     def later(i, carry):
-        @pl.when((me >= i) & (i > 2))
+        @pl.when(me >= i)
         def _():
             arrival(i - 1).wait_recv()
 
@@ -319,16 +330,14 @@
             def _():
                 ring(i).start()
 
-        @pl.when(me >= i)
-        def _():
             prefill_block(me - i, False)
         return carry
 
-    lax.fori_loop(2, n, later, 0)
+    lax.fori_loop(3, n, later, 0)
 
     unit = jnp.where(iota((tok, tok), 0) == iota((tok, tok), 1), 1.0, 0.0).astype(jnp.bfloat16)
     for at in range(q_heads // pair):
-        done = (mix_ref[at] / total_ref[at, 0:1, :]).astype(jnp.bfloat16)
+        done = (mix_ref[at] * (1.0 / total_ref[at, 0:1, :])).astype(jnp.bfloat16)
         for i in range(pair):
             turned = nt_dot(unit, done[:, i * tok:(i + 1) * tok])
             head = at * pair + i

time: 19.6 us -> 19.5 us (level)
  no operation moved by 1% of the time
where the time goes in v4:
time: 19.5 us; the launch traced here: 19.4 us
  Pallas kernels  18.8 us (96%)
  between operations  0.64 us (3%)
    pallas_call x1, Pallas kernels, local(): pl.pallas_call(functools.partial(kernel, n, nb, page_rows, w_chunks), out...  17.9 us
    pallas_call x1, Pallas kernels, local(): pl.pallas_call(hand_over, out_shape=(pltpu.HBM(pre_out.shape, pre_out.dty...  0.81 us

profile of v4, /device:TPU:26, one launch (start us, length us, event | category | flops | bytes accessed | tf_op | source)
XLA Modules:
  0.0 19.4 jit_solution(14511261633059030698)
XLA Ops:
  0.6 17.9 %prefill_and_decode.1 = (bf16[1,128,2048]{2,1,0:T(8,128)(2,1)S(1)}, f32[3,2,2048]{2,1,0:T(2,128)S(1)}) custom-call(s32[1,1,8]{2,1,0:T(1,128)} %bitcast.8, s32[2,4]{1,0:T(2,128)} %tab_hbm.1, s32[2]{0:T(128)} %len_hbm.1, bf16[1,128,256]{2,1,0:T(8,128)(2,1)} %k_hbm.1, bf16[1,128,256]{2,1,0:T(8,128)(2,1)} %v_hbm.1, bf16[8,16,256]{2,1,0:T(8,128)(2,1)} %ck_hbm.1, ...), custom_call_target="tpu_custom_call" | custom-call | tf_op jit(solution)/shard_map/prefill_and_decode/pallas_call | solution.py:387
  18.6 0.8 %hand_over.1 = (bf16[1,128,2048]{2,1,0:T(8,128)(2,1)}, f32[3,2,2048]{2,1,0:T(2,128)}) custom-call(bf16[1,128,2048]{2,1,0:T(8,128)(2,1)S(1)} %get-tuple-element.6.pre_ref, f32[3,2,2048]{2,1,0:T(2,128)S(1)} %get-tuple-element.7.dec_ref), custom_call_target="tpu_custom_call" | custom-call | tf_op jit(solution)/shard_map/hand_over/pallas_call | solution.py:435

commit v5 on v4

--- a/solution.py
+++ b/solution.py
@@ -140,22 +140,33 @@
                 recv_sem=page_rs.at[k - 1], device_id={"batch": since}, device_id_type=pl.DeviceIdType.MESH),
         )
 
+    even = lax.rem(me, 2) == 0
+
+    def two_up():
+        return pltpu.make_async_remote_copy(
+            src_ref=kv.at[me], dst_ref=kv.at[me], send_sem=ring_send.at[n - 1], recv_sem=ring_recv.at[1],
+            device_id={"seq": me + 2}, device_id_type=pl.DeviceIdType.MESH)
+
     @pl.when(me < n - 1)
     def _():
         ring(0).start()
 
+    @pl.when(even & (me < n - 2))
+    def _():
+        two_up().start()
+
     for k in range(1, nb):
         for copy in page_pair(k):
             copy.start()
 
     def relay(i):
-        @pl.when((me > i) & (me < n - 1))
+        @pl.when((me > i) & (me < n - 1) & (even | (i > 0)))
         def _():
             arrival(i).wait_recv()
             ring(i + 1).start()
 
-    def last_arrival(i):
-        @pl.when(me == n - 1)
+    def final_arrival(i):
+        @pl.when((me > i) & ((me == n - 1) | (~even & (i == 0))))
         def _():
             arrival(i).wait_recv()
 
@@ -282,15 +293,16 @@
         for copy in partial_pair(k, me, lax.rem(me + k, n)):
             copy.start()
 
-    last_arrival(0)
+    if n > 2:
+        relay(1)
+    final_arrival(0)
 
     @pl.when(me >= 1)
     def _():
         prefill_block(me - 1, False)
 
     if n > 2:
-        relay(1)
-        last_arrival(1)
+        final_arrival(1)
 
         @pl.when(me >= 2)
         def _():
@@ -350,9 +362,13 @@
             dec_ref[m, :, c * step:(c + 1) * step] = y[m * requests:(m + 1) * requests]
 
     for i in range(n - 1):
-        @pl.when((me < n - 1) & (me >= i))
+        @pl.when((me < n - 1) & (me >= i) & (even | (i != 1)))
         def _():
             ring(i).wait_send()
+
+    @pl.when(even & (me < n - 2))
+    def _():
+        two_up().wait_send()
     for k in range(1, nb):
         for copy in page_pair(k):
             copy.wait_send()
@@ -419,7 +435,7 @@
             pltpu.VMEM((w_chunks, ROWS, out_columns // w_chunks), jnp.float32),
             pltpu.VMEM((w_chunks, ROWS, out_columns // w_chunks), jnp.float32),
             dma((12,)),
-            dma((n - 1,)), dma((n - 1,)),
+            dma((n,)), dma((n - 1,)),
             dma((nb - 1,)), dma((nb - 1,)), dma((nb - 1,)), dma((nb - 1,)),
             dma((n - 1,)), dma((n - 1,)), dma((n - 1,)), dma((n - 1,)),
             dma((w_chunks,)), dma((w_chunks,)),

time: 19.5 us -> 18.8 us (0.964)
  the two profiles are of different devices: /device:TPU:26 before, /device:TPU:0 now
where the time goes in v5:
time: 18.8 us; the launch traced here: 18.6 us
  Pallas kernels  18 us (96%)
  between operations  0.64 us (3%)
    pallas_call x1, Pallas kernels, local(): pl.pallas_call(functools.partial(kernel, n, nb, page_rows, w_chunks), out...  17.2 us
    pallas_call x1, Pallas kernels, local(): pl.pallas_call(hand_over, out_shape=(pltpu.HBM(pre_out.shape, pre_out.dty...  0.81 us

profile of v5, /device:TPU:0, one launch (start us, length us, event | category | flops | bytes accessed | tf_op | source)
XLA Modules:
  0.0 18.6 jit_solution(17390270096745190441)
XLA Ops:
  0.6 17.2 %prefill_and_decode.1 = (bf16[1,128,2048]{2,1,0:T(8,128)(2,1)S(1)}, f32[3,2,2048]{2,1,0:T(2,128)S(1)}) custom-call(s32[1,1,8]{2,1,0:T(1,128)} %bitcast.8, s32[2,4]{1,0:T(2,128)} %tab_hbm.1, s32[2]{0:T(128)} %len_hbm.1, bf16[1,128,256]{2,1,0:T(8,128)(2,1)} %k_hbm.1, bf16[1,128,256]{2,1,0:T(8,128)(2,1)} %v_hbm.1, bf16[8,16,256]{2,1,0:T(8,128)(2,1)} %ck_hbm.1, ...), custom_call_target="tpu_custom_call" | custom-call | tf_op jit(solution)/shard_map/prefill_and_decode/pallas_call | solution.py:403
  17.8 0.8 %hand_over.1 = (bf16[1,128,2048]{2,1,0:T(8,128)(2,1)}, f32[3,2,2048]{2,1,0:T(2,128)}) custom-call(bf16[1,128,2048]{2,1,0:T(8,128)(2,1)S(1)} %get-tuple-element.6.pre_ref, f32[3,2,2048]{2,1,0:T(2,128)S(1)} %get-tuple-element.7.dec_ref), custom_call_target="tpu_custom_call" | custom-call | tf_op jit(solution)/shard_map/hand_over/pallas_call | solution.py:451

commit v6 on v5

--- a/solution.py
+++ b/solution.py
@@ -212,6 +212,27 @@
     causal = (key_token % requests == request) & (key_token <= token) & (me == 0)
     score_new = jnp.where(causal, score_new, floor_score)
 
+    early_peak = jnp.maximum(jnp.max(score_cache, axis=0, keepdims=True), jnp.max(score_new, axis=0, keepdims=True))
+    weight_cache = jnp.where(live > 0, jnp.exp(score_cache - early_peak), 0.0)
+    weight_new = jnp.where(causal, jnp.exp(score_new - early_peak), 0.0)
+    early_total = jnp.sum(weight_cache, axis=0, keepdims=True) + jnp.sum(weight_new, axis=0, keepdims=True)
+
+    def dec_values(values, weights):
+        both = tn_dot(values, jnp.concatenate(halves(weights), axis=1))
+        return both[:, :lanes] + both[:, lanes:]
+
+    lane_head = iota((HD, lanes), 1) // per_head
+
+    def own_head(mixed):
+        acc = mixed[0:HD]
+        for a in range(1, k_heads):
+            acc = jnp.where(lane_head == a, mixed[a * HD:(a + 1) * HD], acc)
+        return acc
+
+    early_acc = own_head(
+        dec_values(cv_ref[...].reshape(cache_rows, kw), weight_cache)
+        + dec_values(new_v, jnp.concatenate([weight_new, weight_new], axis=0)))
+
     pair = 2
     pair_lanes = pair * tok
     sharpness = scaling * LOG2E
@@ -255,26 +276,11 @@
     place_of = iota((wide, lanes), 0) // page_rows
     kept = jnp.concatenate([jnp.where(place_of < count_recv[b][0:1, :], 1, 0) for b in range(nb)], axis=0)
     score_recv = jnp.where(kept > 0, score_recv, floor_score)
-    peak = jnp.maximum(
-        jnp.maximum(jnp.max(score_cache, axis=0, keepdims=True), jnp.max(score_recv, axis=0, keepdims=True)),
-        jnp.max(score_new, axis=0, keepdims=True))
-    weight_cache = jnp.where(live > 0, jnp.exp(score_cache - peak), 0.0)
+    peak = jnp.maximum(early_peak, jnp.max(score_recv, axis=0, keepdims=True))
     weight_recv = jnp.where(kept > 0, jnp.exp(score_recv - peak), 0.0)
-    weight_new = jnp.where(causal, jnp.exp(score_new - peak), 0.0)
-    total = (jnp.sum(weight_cache, axis=0, keepdims=True) + jnp.sum(weight_recv, axis=0, keepdims=True)
-             + jnp.sum(weight_new, axis=0, keepdims=True))
-
-    def dec_values(values, weights):
-        both = tn_dot(values, jnp.concatenate(halves(weights), axis=1))
-        return both[:, :lanes] + both[:, lanes:]
-
-    mixed = dec_values(cv_ref[...].reshape(cache_rows, kw), weight_cache)
-    mixed = mixed + dec_values(received[:, kw:], weight_recv)
-    mixed = mixed + dec_values(new_v, jnp.concatenate([weight_new, weight_new], axis=0))
-    lane_head = iota((HD, lanes), 1) // per_head
-    acc = mixed[0:HD]
-    for a in range(1, k_heads):
-        acc = jnp.where(lane_head == a, mixed[a * HD:(a + 1) * HD], acc)
+    carried = jnp.exp(early_peak - peak)
+    total = early_total * carried + jnp.sum(weight_recv, axis=0, keepdims=True)
+    acc = early_acc * carried + own_head(dec_values(received[:, kw:], weight_recv))
     acc_all[me] = acc.astype(jnp.bfloat16)
     stat_row = iota((ROWS, lanes), 0)
     stat_all[me] = jnp.where(stat_row == 0, peak, total)
@@ -307,6 +313,19 @@
         @pl.when(me >= 2)
         def _():
             prefill_block(me - 2, False)
+
+    def finish():
+        unit = jnp.where(iota((tok, tok), 0) == iota((tok, tok), 1), 1.0, 0.0).astype(jnp.bfloat16)
+        for at in range(q_heads // pair):
+            done = (mix_ref[at] * (1.0 / total_ref[at, 0:1, :])).astype(jnp.bfloat16)
+            for i in range(pair):
+                turned = nt_dot(unit, done[:, i * tok:(i + 1) * tok])
+                head = at * pair + i
+                out_ref[0, :, head * HD:(head + 1) * HD] = turned.astype(jnp.bfloat16)
+
+    @pl.when(me <= 1)
+    def _():
+        finish()
 
     for k in range(1, n):
         since = lax.rem(me - k + n, n)
@@ -347,13 +366,9 @@
 
     lax.fori_loop(3, n, later, 0)
 
-    unit = jnp.where(iota((tok, tok), 0) == iota((tok, tok), 1), 1.0, 0.0).astype(jnp.bfloat16)
-    for at in range(q_heads // pair):
-        done = (mix_ref[at] * (1.0 / total_ref[at, 0:1, :])).astype(jnp.bfloat16)
-        for i in range(pair):
-            turned = nt_dot(unit, done[:, i * tok:(i + 1) * tok])
-            head = at * pair + i
-            out_ref[0, :, head * HD:(head + 1) * HD] = turned.astype(jnp.bfloat16)
+    @pl.when(me > 1)
+    def _():
+        finish()
 
     for c in range(w_chunks):
         y_copy(c).wait()

time: 18.8 us -> 18.7 us (level)
  no operation moved by 1% of the time
where the time goes in v6:
time: 18.7 us; the launch traced here: 18.5 us
  Pallas kernels  17.9 us (96%)
  between operations  0.64 us (3%)
    pallas_call x1, Pallas kernels, local(): pl.pallas_call(functools.partial(kernel, n, nb, page_rows, w_chunks), out...  17.1 us
    pallas_call x1, Pallas kernels, local(): pl.pallas_call(hand_over, out_shape=(pltpu.HBM(pre_out.shape, pre_out.dty...  0.81 us

profile of v6, /device:TPU:0, one launch (start us, length us, event | category | flops | bytes accessed | tf_op | source)
XLA Modules:
  0.0 18.5 jit_solution(6509310667773895183)
XLA Ops:
  0.6 17.1 %prefill_and_decode.1 = (bf16[1,128,2048]{2,1,0:T(8,128)(2,1)S(1)}, f32[3,2,2048]{2,1,0:T(2,128)S(1)}) custom-call(s32[1,1,8]{2,1,0:T(1,128)} %bitcast.8, s32[2,4]{1,0:T(2,128)} %tab_hbm.1, s32[2]{0:T(128)} %len_hbm.1, bf16[1,128,256]{2,1,0:T(8,128)(2,1)} %k_hbm.1, bf16[1,128,256]{2,1,0:T(8,128)(2,1)} %v_hbm.1, bf16[8,16,256]{2,1,0:T(8,128)(2,1)} %ck_hbm.1, ...), custom_call_target="tpu_custom_call" | custom-call | tf_op jit(solution)/shard_map/prefill_and_decode/pallas_call | solution.py:418
  17.7 0.8 %hand_over.1 = (bf16[1,128,2048]{2,1,0:T(8,128)(2,1)}, f32[3,2,2048]{2,1,0:T(2,128)}) custom-call(bf16[1,128,2048]{2,1,0:T(8,128)(2,1)S(1)} %get-tuple-element.6.pre_ref, f32[3,2,2048]{2,1,0:T(2,128)S(1)} %get-tuple-element.7.dec_ref), custom_call_target="tpu_custom_call" | custom-call | tf_op jit(solution)/shard_map/hand_over/pallas_call | solution.py:466
